TPU v7x, 256 devices: a whole 4x4x8 slice. The times are simulated.
256 devices in a mesh: dp: 16 (over x, y_hi, core), seq: 16 (over z, y_lo).
Axes of the slice: x: 4, y: 4 (y_hi: 2, y_lo: 2; y = y_hi * 2 + y_lo), z: 8, core: 2. Of those that a mesh axis runs over, the one named last changes fastest.
Arguments:
- coarse: bfloat16 [16, 4096, 1024], P('dp', 'seq'), may hold values from -6 to 6
- skip: bfloat16 [16, 8192, 768], P('dp', 'seq'), may hold values from -6 to 6
- conv_weight: bfloat16 [5, 1024, 768], replicated, may hold values from -0.078125 to 0.078125
- donor_weight: bfloat16 [768, 768], replicated, may hold values from -0.21875 to 0.21875
- acceptor_weight: bfloat16 [768, 768], replicated, may hold values from -0.21875 to 0.21875
- other_grad: bfloat16 [16, 8192, 768], P('dp', 'seq'), may hold values from -4 to 4
- score_grad: float32 [16, 1024], P('dp', 'seq'), may hold values from -16 to 16
- donor_pos: int32 [16, 1024], P('dp', 'seq'), may hold values from 0 to 511
- acceptor_pos: int32 [16, 1024], P('dp', 'seq'), may hold values from 0 to 8191, as said below
- pair_mask: int32 [16, 1024], P('dp', 'seq'), may hold values 0 or 1
Outputs:
- scores: float32 [16, 1024], P('dp', 'seq')
- coarse_grad: bfloat16 [16, 4096, 1024], P('dp', 'seq')
- donor_weight_grad: float32 [768, 768], P('seq')
- acceptor_weight_grad: float32 [768, 768], P('seq')
Inputs may be any that keep to these rules, and one draw needn't show every extreme that they name: Position in the whole sample. Among the 64 slots held by one shard of a sample, at most 8 have their acceptor on any one shard (shard = acceptor_pos // 512); in every sample some shard is named by exactly 8 slots of every shard.
All inputs are finite; a program needn't handle non-finite values. No bound on the sum of `pair_mask` on one device may be relied on, other than what follows from the above.
Results may differ from a plain program's by a relative error of at most 0.013.
Values may be sent and summed in bfloat16 or wider, within the bound.
A program may use at most 128 MiB of HBM per device.

v0:
```python
import math
import jax
import jax.numpy as jnp
from jax import lax
from jax.sharding import PartitionSpec as P

ACAP = 8


def with_halo(cells, sides, width):
    for axis, dim in sides:
        count = lax.axis_size(axis)
        ends = count - 1
        head = lax.slice_in_dim(cells, 0, width, axis=dim)
        tail = lax.slice_in_dim(cells, cells.shape[dim] - width, cells.shape[dim], axis=dim)
        cells = jnp.concatenate(
            [
                lax.ppermute(tail, axis, [(i, (i + 1) % count) for i in range(ends)]),
                cells,
                lax.ppermute(head, axis, [((i + 1) % count, i) for i in range(ends)]),
            ],
            axis=dim,
        )
    return cells


def activate(values):
    return jax.nn.gelu(values, approximate=True)


def on_device(
    coarse,
    skip,
    conv_weight,
    donor_weight,
    acceptor_weight,
    other_grad,
    score_grad,
    donor_pos,
    acceptor_pos,
    pair_mask,
):
    seq_count = lax.axis_size("seq")
    batch_count = lax.axis_size("dp")
    taps = conv_weight.shape[0]
    emb_width = donor_weight.shape[1]
    inverse_root = 1.0 / math.sqrt(emb_width)
    widened = with_halo(coarse, (("seq", 1),), 1)
    upsampled = jnp.repeat(widened[0], 2, axis=0)
    row_count = upsampled.shape[0] - 4
    preact = skip[0].astype(jnp.float32)
    for shift_index in range(taps):
        preact = preact + jnp.dot(
            upsampled[shift_index : shift_index + row_count],
            conv_weight[shift_index],
            preferred_element_type=jnp.float32,
        )
    activated = activate(preact).astype(jnp.bfloat16)
    donor_rows = donor_pos[0]
    donor_act = activated[donor_rows]
    donor_emb = jnp.dot(donor_act, donor_weight, preferred_element_type=jnp.float32).astype(
        jnp.bfloat16
    )
    targets = acceptor_pos[0]
    owner = targets // row_count
    local_row = targets % row_count
    owner_hits = (owner[:, None] == jnp.arange(seq_count, dtype=jnp.int32)[None, :]).astype(
        jnp.int32
    )
    place_rank = jnp.sum((jnp.cumsum(owner_hits, axis=0) - owner_hits) * owner_hits, axis=1)
    capacity = ACAP
    slot_index = owner * capacity + place_rank
    requests = (
        jnp.zeros((seq_count * capacity,), jnp.int32)
        .at[slot_index]
        .set(local_row)
        .reshape(seq_count, capacity)
    )
    received = lax.all_to_all(requests, "seq", split_axis=0, concat_axis=0, tiled=True)
    wanted = activated[received.reshape(-1)]
    projected = jnp.dot(wanted, acceptor_weight, preferred_element_type=jnp.float32).astype(
        jnp.bfloat16
    )
    projected = projected.reshape(received.shape[0], received.shape[1], emb_width)
    returned = lax.all_to_all(projected, "seq", split_axis=0, concat_axis=0, tiled=True)
    returned, served_rows = (returned, received)
    acceptor_emb = returned.reshape(seq_count * capacity, emb_width)[slot_index]
    mask_float = pair_mask[0].astype(jnp.float32)
    scores = (
        mask_float
        * jnp.sum(donor_emb.astype(jnp.float32) * acceptor_emb.astype(jnp.float32), axis=1)
        * inverse_root
    )
    weighted = score_grad[0] * mask_float
    donor_emb_grad = (weighted[:, None] * acceptor_emb.astype(jnp.float32) * inverse_root).astype(
        jnp.bfloat16
    )
    acceptor_emb_grad = (weighted[:, None] * donor_emb.astype(jnp.float32) * inverse_root).astype(
        jnp.bfloat16
    )
    outgoing = (
        jnp.zeros((seq_count * capacity, emb_width), jnp.bfloat16)
        .at[slot_index]
        .set(acceptor_emb_grad)
    )
    outgoing = outgoing.reshape(seq_count, capacity, emb_width)
    received = lax.all_to_all(outgoing, "seq", split_axis=0, concat_axis=0, tiled=True)
    flattened = received.reshape(-1, emb_width)
    to_rows = jnp.dot(flattened, acceptor_weight.T, preferred_element_type=jnp.float32)
    row_terms = to_rows.reshape(received.shape[0], received.shape[1], -1)
    served_flat = served_rows.reshape(-1)
    act_grad = other_grad[0].astype(jnp.float32)
    act_grad = act_grad.at[donor_rows].add(
        jnp.dot(donor_emb_grad, donor_weight.T, preferred_element_type=jnp.float32)
    )
    act_grad = act_grad.at[served_flat].add(row_terms.reshape(-1, row_terms.shape[2]))
    pull = jax.vjp(activate, preact)[1]
    preact_grad = pull(act_grad)[0].astype(jnp.bfloat16)
    widened_grad = with_halo(preact_grad[None], (("seq", 1),), 2)[0]
    upsampled_grad = jnp.zeros((row_count, conv_weight.shape[1]), jnp.float32)
    for shift_index in range(taps):
        begin = 4 - shift_index
        upsampled_grad = upsampled_grad + jnp.dot(
            widened_grad[begin : begin + row_count],
            conv_weight[shift_index].T,
            preferred_element_type=jnp.float32,
        )
    coarse_grad = (
        upsampled_grad.reshape(row_count // 2, 2, -1).sum(axis=1).astype(jnp.bfloat16)[None]
    )
    served_act = activated[served_flat]
    served_emb_grad = received.reshape(-1, emb_width)
    rows_each = donor_weight.shape[0] // seq_count
    factor = 1.0 / batch_count
    donor_term = jnp.dot(donor_act.T, donor_emb_grad, preferred_element_type=jnp.float32)
    acceptor_term = jnp.dot(served_act.T, served_emb_grad, preferred_element_type=jnp.float32)
    donor_total, acceptor_total = lax.psum((donor_term, acceptor_term), ("dp", "seq"))
    first_row = lax.axis_index("seq") * rows_each
    donor_part = lax.dynamic_slice_in_dim(donor_total, first_row, rows_each, 0)
    acceptor_part = lax.dynamic_slice_in_dim(acceptor_total, first_row, rows_each, 0)
    return (scores[None], coarse_grad, donor_part * factor, acceptor_part * factor)


def solution(mesh):
    in_specs = (
        P("dp", "seq", None),
        P("dp", "seq", None),
        P(),
        P(),
        P(),
        P("dp", "seq", None),
        P("dp", "seq"),
        P("dp", "seq"),
        P("dp", "seq"),
        P("dp", "seq"),
    )
    out_specs = (P("dp", "seq"), P("dp", "seq", None), P("seq", None), P("seq", None))
    return jax.shard_map(
        on_device, mesh=mesh, in_specs=in_specs, out_specs=out_specs, check_vma=False
    )
```

profile of v0, /device:TPU:2, one launch (start us, length us, event | category | flops | bytes accessed | tf_op | source)
XLA Modules:
  0.0 379.7 jit_solution(3904731837600903716)
XLA Ops:
  8.0 3.5 collective-permute-start
  16.0 11.7 %all-to-all-start = ((s32[16,1,8]{2,1,0:T(1,128)}), s32[16,1,8]{2,1,0:T(1,128)S(1)}, u32[]{:S(2)}, u32[]{:S(2)}) async-start(s32[16,1,8]{2,1,0:T(1,128)} %bitcast.16), calls=%async_computation | async-start | bytes 16384 | tf_op jit(solution)/shard_map/all_to_all | solution.py:79
  27.8 1.6 broadcast_in_dim.14
  29.8 3.6 fusion.20
  33.4 2.7 all-to-all-done
  38.2 1.4 reshape.227
  39.6 4.0 %fusion.16 = f32[512,768]{1,0:T(8,128)} fusion(bf16[5,1024,768]{2,1,0:T(8,128)(2,1)} %param.12, bf16[516,1024]{1,0:T(8,128)(2,1)} %reshape.227), kind=kOutput, calls=%fused_computation.27 | convolution fusion | flops 805306368 | bytes 4194304 | tf_op jit(solution)/shard_map/dot_general | solution.py:53
  43.6 3.6 fusion.24
  49.1 3.6 fusion.12
  53.7 6.1 %multiply_convert_fusion = (bf16[512,768]{1,0:T(8,128)(2,1)S(1)}, f32[512,768]{1,0:T(8,128)}) fusion(f32[512,768]{1,0:T(8,128)} %fusion.12, f32[512,768]{1,0:T(8,128)} %fusion.16, f32[512,768]{1,0:T(8,128)} %fusion.20, f32[512,768]{1,0:T(8,128)} %fusion.24, bf16[512,1024]{1,0:T(8,128)(2,1)S(1)} %slice.101, bf16[5,1024,768]{2,1,0:T(8,128)(2,1)} %param.12, ...), kind=kOutput, calls=%fused_computation.41 | convolution fusion | flops 811204608 | bytes 12058624 | tf_op jit(solution)/shard_map/dot_general | solution.py:53
  61.7 5.4 %all-to-all-start.1 = ((bf16[16,8,768]{2,1,0:T(8,128)(2,1)}), bf16[16,8,768]{2,1,0:T(8,128)(2,1)}, u32[]{:S(2)}, u32[]{:S(2)}) async-start(bf16[16,8,768]{2,1,0:T(8,128)(2,1)} %fusion.40), calls=%async_computation.1 | async-start | bytes 393216 | tf_op jit(solution)/shard_map/all_to_all | solution.py:85
  69.8 7.8 %all-to-all-done.1 = bf16[16,8,768]{2,1,0:T(8,128)(2,1)} async-done(((bf16[16,8,768]{2,1,0:T(8,128)(2,1)}), bf16[16,8,768]{2,1,0:T(8,128)(2,1)}, u32[]{:S(2)}, u32[]{:S(2)}) %all-to-all-start.1) | async-done | bytes 196640 | tf_op jit(solution)/shard_map/all_to_all | solution.py:85
  77.5 1.7 gather_fusion.2
  79.3 1.8 fusion.60
  81.6 1.7 scatter_custom_fusion.2
  83.3 3.5 all-to-all-start.2
  87.0 1.8 fusion.74
  88.8 1.6 scatter_fusion
  90.4 1.9 fusion.72
  92.4 4.5 %all-to-all-done.2 = bf16[16,8,768]{2,1,0:T(8,128)(2,1)S(1)} async-done(((bf16[16,8,768]{2,1,0:T(8,128)(2,1)}), bf16[16,8,768]{2,1,0:T(8,128)(2,1)S(1)}, u32[]{:S(2)}, u32[]{:S(2)}) %all-to-all-start.2) | async-done | bytes 196640 | tf_op jit(solution)/shard_map/all_to_all | solution.py:107
  98.2 2.5 scatter_fusion.1
  100.6 2.0 fusion.63
  102.7 2.6 fusion.6
  105.3 1.6 collective-permute-start.2
  106.9 2.4 fusion.18
  109.3 4.5 %collective-permute-start.3 = (bf16[1,2,768]{2,1,0:T(2,128)(2,1)S(1)}, bf16[1,2,768]{2,1,0:T(2,128)(2,1)S(1)}, u32[]{:S(2)}, u32[]{:S(2)}) collective-permute-start(bf16[1,2,768]{2,1,0:T(2,128)(2,1)S(1)} %get-tuple-element.7), channel_id=1, source_target_pairs={{0,1},{1,2},{2,3},{3,4},{4,5},{5,6},{6,7},{7,8},{8,9},{9,10},{10,1... | collective-permute-start | bytes 9224 | tf_op jit(solution)/shard_map/ppermute | solution.py:18
  113.9 2.4 fusion.26
  118.4 2.4 add_add_fusion
  120.8 2.5 reshape.233
  123.3 3.6 reduce_sum.35
  126.9 244.2 %all-reduce.3.cloned.1.call-done = (f32[768,768]{1,0:T(8,128)}, f32[768,768]{1,0:T(8,128)}) async-done(((f32[768,768]{1,0:T(8,128)}, f32[768,768]{1,0:T(8,128)}), (f32[768,768]{1,0:T(8,128)}, f32[768,768]{1,0:T(8,128)})) %all-reduce.3.cloned.1.call-update) | async-done | bytes 4718608 | tf_op jit(solution)/shard_map/psum | solution.py:137
  371.1 1.7 dynamic-slice_multiply_fusion
  (67 shorter events, 19.3 us)
Async XLA Ops:
  7.2 53.5 %copy-start = (bf16[768,768]{1,0:T(8,128)(2,1)S(1)}, bf16[768,768]{1,0:T(8,128)(2,1)}, u32[]{:S(2)}) copy-start(bf16[768,768]{1,0:T(8,128)(2,1)} %param.14) | copy-start | bytes 3538948
  8.0 29.4 %collective-permute-start = (bf16[1,1,1024]{2,1,0:T(2,128)(2,1)S(1)}, bf16[1,1,1024]{2,1,0:T(2,128)(2,1)S(1)}, u32[]{:S(2)}, u32[]{:S(2)}) collective-permute-start(bf16[1,1,1024]{2,1,0:T(2,128)(2,1)S(1)} %get-tuple-element.10), channel_id=1, source_target_pairs={{0,1},{1,2},{2,3},{3,4},{4,5},{5,6},{6,7},{7,8},{8,9},{9,10},{10,1... | collective-permute-start | bytes 6152 | tf_op jit(solution)/shard_map/ppermute | solution.py:18
  11.5 26.0 %collective-permute-start.1 = (bf16[1,1,1024]{2,1,0:T(2,128)(2,1)S(1)}, bf16[1,1,1024]{2,1,0:T(2,128)(2,1)S(1)}, u32[]{:S(2)}, u32[]{:S(2)}) collective-permute-start(bf16[1,1,1024]{2,1,0:T(2,128)(2,1)S(1)} %get-tuple-element.11), channel_id=1, source_target_pairs={{1,0},{2,1},{3,2},{4,3},{5,4},{6,5},{7,6},{8,7},{9,8},{10,9},{11,1... | collective-permute-start | bytes 6152 | tf_op jit(solution)/shard_map/ppermute | solution.py:20
  14.5 18.9 %copy-start.9 = (s32[64]{0:T(128)}, s32[64]{0:T(128)S(1)}, u32[]{:S(2)}) copy-start(s32[64]{0:T(128)S(1)} %fusion.77) | copy-start | bytes 772
  16.0 20.2 %all-to-all-start = ((s32[16,1,8]{2,1,0:T(1,128)}), s32[16,1,8]{2,1,0:T(1,128)S(1)}, u32[]{:S(2)}, u32[]{:S(2)}) async-start(s32[16,1,8]{2,1,0:T(1,128)} %bitcast.16), calls=%async_computation | async-start | bytes 16384 | tf_op jit(solution)/shard_map/all_to_all | solution.py:79
  27.7 2.1 copy-start.10
  29.8 7.7 %copy-start.1 = (bf16[1,256,1024]{2,1,0:T(8,128)(2,1)S(1)}, bf16[1,256,1024]{2,1,0:T(8,128)(2,1)}, u32[]{:S(2)}) copy-start(bf16[1,256,1024]{2,1,0:T(8,128)(2,1)} %param.10) | copy-start | bytes 1572868
  39.6 4.0 %copy-start.5 = (bf16[516,1024]{1,0:T(8,128)(2,1)S(1)}, bf16[516,1024]{1,0:T(8,128)(2,1)}, u32[]{:S(2)}) copy-start(bf16[516,1024]{1,0:T(8,128)(2,1)} %reshape.227) | copy-start | bytes 3170308
  49.1 3.6 copy-start.2
  60.7 6.5 %copy-start.3 = (bf16[128,768]{1,0:T(8,128)(2,1)}, bf16[128,768]{1,0:T(8,128)(2,1)S(1)}, u32[]{:S(2)}) copy-start(bf16[128,768]{1,0:T(8,128)(2,1)S(1)} %gather_fusion.1) | copy-start | bytes 589828
  61.7 15.8 %all-to-all-start.1 = ((bf16[16,8,768]{2,1,0:T(8,128)(2,1)}), bf16[16,8,768]{2,1,0:T(8,128)(2,1)}, u32[]{:S(2)}, u32[]{:S(2)}) async-start(bf16[16,8,768]{2,1,0:T(8,128)(2,1)} %fusion.40), calls=%async_computation.1 | async-start | bytes 393216 | tf_op jit(solution)/shard_map/all_to_all | solution.py:85
  69.8 11.3 %copy-start.7 = (f32[1,64]{1,0:T(1,128)S(1)}, f32[1,64]{1,0:T(1,128)}, u32[]{:S(2)}) copy-start(f32[1,64]{1,0:T(1,128)} %param.16) | copy-start | bytes 772
  69.8 11.3 %copy-start.8 = (s32[1,64]{1,0:T(1,128)S(1)}, s32[1,64]{1,0:T(1,128)}, u32[]{:S(2)}) copy-start(s32[1,64]{1,0:T(1,128)} %param.19) | copy-start | bytes 772
  83.3 13.6 %all-to-all-start.2 = ((bf16[16,8,768]{2,1,0:T(8,128)(2,1)}), bf16[16,8,768]{2,1,0:T(8,128)(2,1)S(1)}, u32[]{:S(2)}, u32[]{:S(2)}) async-start(bf16[16,8,768]{2,1,0:T(8,128)(2,1)} %bitcast.23), calls=%async_computation.2 | async-start | bytes 393216 | tf_op jit(solution)/shard_map/all_to_all | solution.py:107
  86.8 284.3 %all-reduce.3.cloned.1.call-start = ((), (), s32[]{:S(2)}) async-start(), calls=%async_computation.3 | async-start | bytes 9437184 | tf_op jit(solution)/shard_map/psum | solution.py:137
  88.8 1.6 copy-start.6
  98.2 2.5 copy-start.4
  102.7 13.6 %slice-start = ((s8[7864320]{0:T(1024)(128)(4,1)}), s8[4194304]{0:T(1024)(128)(4,1)S(1)}, s32[]{:S(2)}) async-start(s8[7864320]{0:T(1024)(128)(4,1)} %bitcast.129), calls=%async_computation.4 | async-start | bytes 8388608
  105.3 11.0 %slice-start.1 = ((s8[7864320]{0:T(1024)(128)(4,1)}), s8[3670016]{0:T(1024)(128)(4,1)S(1)}, s32[]{:S(2)}) async-start(s8[7864320]{0:T(1024)(128)(4,1)} %bitcast.129), calls=%async_computation.5 | async-start | bytes 7340032
  105.3 8.5 %collective-permute-start.2 = (bf16[1,2,768]{2,1,0:T(2,128)(2,1)S(1)}, bf16[1,2,768]{2,1,0:T(2,128)(2,1)S(1)}, u32[]{:S(2)}, u32[]{:S(2)}) collective-permute-start(bf16[1,2,768]{2,1,0:T(2,128)(2,1)S(1)} %get-tuple-element.6), channel_id=1, source_target_pairs={{1,0},{2,1},{3,2},{4,3},{5,4},{6,5},{7,6},{8,7},{9,8},{10,9},{11,1... | collective-permute-start | bytes 9224 | tf_op jit(solution)/shard_map/ppermute | solution.py:20
  109.3 8.0 %collective-permute-start.3 = (bf16[1,2,768]{2,1,0:T(2,128)(2,1)S(1)}, bf16[1,2,768]{2,1,0:T(2,128)(2,1)S(1)}, u32[]{:S(2)}, u32[]{:S(2)}) collective-permute-start(bf16[1,2,768]{2,1,0:T(2,128)(2,1)S(1)} %get-tuple-element.7), channel_id=1, source_target_pairs={{0,1},{1,2},{2,3},{3,4},{4,5},{5,6},{6,7},{7,8},{8,9},{9,10},{10,1... | collective-permute-start | bytes 9224 | tf_op jit(solution)/shard_map/ppermute | solution.py:18
Sparse Core Ops, SparseCore 0:
  102.8 268.2 all-reduce.2
where the time goes:
time: 380 us
  waiting for transfers between devices  259 us (68%)
  matrix products  39.8 us (10%)
  starting transfers between devices  31.8 us (8%)
  other arithmetic  18.9 us (5%)
  local copies, waits for them, and re-layouts  15.4 us (4%)
  between operations  14.5 us (4%)
    psum x1, waiting for transfers between devices, on_device(): lax.psum((donor_term, acceptor_term), ('dp', 'seq'))  244 us
    dot_general x5, matrix products, on_device(): jnp.dot(upsampled[shift_index:shift_index + row_count], conv_weight[shift...  20.8 us
    all_to_all x1, starting transfers between devices, on_device(): lax.all_to_all(requests, 'seq', split_axis=0, concat_axis=0, tiled=True)  11.7 us
    dot_general x5, matrix products, on_device(): jnp.dot(widened_grad[begin:begin + row_count], conv_weight[shift_index].T...  9.29 us
    ppermute x2, starting transfers between devices, with_halo(): lax.ppermute(tail, axis, [(i, (i + 1) % count) for i in range(ends)])  8.02 us
    all_to_all x1, waiting for transfers between devices, on_device(): lax.all_to_all(projected, 'seq', split_axis=0, concat_axis=0, tiled=True)  7.75 us
  transfers between devices with their start and end apart: 8, of which 4 were waited for; matrix products, arithmetic and copies ran while one was open for 9% of the time, Pallas kernels for 0%

commit v1 on v0

--- a/solution.py
+++ b/solution.py
@@ -134,7 +134,7 @@
     factor = 1.0 / batch_count
     donor_term = jnp.dot(donor_act.T, donor_emb_grad, preferred_element_type=jnp.float32)
     acceptor_term = jnp.dot(served_act.T, served_emb_grad, preferred_element_type=jnp.float32)
-    donor_total, acceptor_total = lax.psum((donor_term, acceptor_term), ("dp", "seq"))
+    donor_total, acceptor_total = lax.psum(lax.psum((donor_term, acceptor_term), "seq"), "dp")
     first_row = lax.axis_index("seq") * rows_each
     donor_part = lax.dynamic_slice_in_dim(donor_total, first_row, rows_each, 0)
     acceptor_part = lax.dynamic_slice_in_dim(acceptor_total, first_row, rows_each, 0)

time: 380 us -> 488 us (1.28); the launches traced: 380 us -> 481 us
  waiting for transfers between devices: 259 us -> 363 us
    psum x1 -> x2, waiting for transfers between devices: 244 us -> 344 us  [the longest x1 218 us: on_device(): lax.psum((donor_term, acceptor_term), 'seq')]
  transfers between devices with their start and end apart: 8 -> 9, of which waited for: 4 -> 5; matrix products, arithmetic and copies ran while one was open for 9% -> 8% of each run, Pallas kernels for 0% -> 0%
where the time goes in v1:
time: 488 us; the launch traced here: 481 us
  waiting for transfers between devices  363 us (74%)
  matrix products  38.7 us (8%)
  starting transfers between devices  31.8 us (7%)
  other arithmetic  19.1 us (4%)
  between operations  14.4 us (3%)
  local copies, waits for them, and re-layouts  14.3 us (3%)
    psum x1, waiting for transfers between devices, on_device(): lax.psum((donor_term, acceptor_term), 'seq')  218 us
    psum x1, waiting for transfers between devices, on_device(): lax.psum(lax.psum((donor_term, acceptor_term), 'seq'), 'dp')  126 us
    dot_general x5, matrix products, on_device(): jnp.dot(upsampled[shift_index:shift_index + row_count], conv_weight[shift...  20.8 us
    all_to_all x1, starting transfers between devices, on_device(): lax.all_to_all(requests, 'seq', split_axis=0, concat_axis=0, tiled=True)  11.7 us
  transfers between devices with their start and end apart: 9, of which 5 were waited for; matrix products, arithmetic and copies ran while one was open for 8% of the time, Pallas kernels for 0%

profile of v1, /device:TPU:2, one launch (start us, length us, event | category | flops | bytes accessed | tf_op | source)
XLA Modules:
  0.0 481.5 jit_solution(10795472511092056501)
XLA Ops:
  8.0 3.5 collective-permute-start
  16.0 11.7 %all-to-all-start = ((s32[16,1,8]{2,1,0:T(1,128)}), s32[16,1,8]{2,1,0:T(1,128)S(1)}, u32[]{:S(2)}, u32[]{:S(2)}) async-start(s32[16,1,8]{2,1,0:T(1,128)} %bitcast.16), calls=%async_computation | async-start | bytes 16384 | tf_op jit(solution)/shard_map/all_to_all | solution.py:79
  27.7 1.6 broadcast_in_dim.14
  29.8 3.6 fusion.20
  33.4 2.8 all-to-all-done
  38.2 1.4 reshape.227
  39.6 4.0 fusion.16
  43.6 3.6 fusion.24
  49.1 3.6 fusion.12
  53.7 6.1 %multiply_convert_fusion = (bf16[512,768]{1,0:T(8,128)(2,1)S(1)}, f32[512,768]{1,0:T(8,128)}) fusion(f32[512,768]{1,0:T(8,128)} %fusion.12, f32[512,768]{1,0:T(8,128)} %fusion.16, f32[512,768]{1,0:T(8,128)} %fusion.20, f32[512,768]{1,0:T(8,128)} %fusion.24, bf16[512,1024]{1,0:T(8,128)(2,1)S(1)} %slice.101, bf16[5,1024,768]{2,1,0:T(8,128)(2,1)} %param.12, ...), kind=kOutput, calls=%fused_computation.41 | convolution fusion | flops 811204608 | bytes 12058624 | tf_op jit(solution)/shard_map/dot_general | solution.py:53
  61.7 5.3 %all-to-all-start.1 = ((bf16[16,8,768]{2,1,0:T(8,128)(2,1)}), bf16[16,8,768]{2,1,0:T(8,128)(2,1)S(1)}, u32[]{:S(2)}, u32[]{:S(2)}) async-start(bf16[16,8,768]{2,1,0:T(8,128)(2,1)} %fusion.40), calls=%async_computation.1 | async-start | bytes 393216 | tf_op jit(solution)/shard_map/all_to_all | solution.py:85
  67.8 1.3 gather_fusion
  69.1 8.3 %all-to-all-done.1 = bf16[16,8,768]{2,1,0:T(8,128)(2,1)S(1)} async-done(((bf16[16,8,768]{2,1,0:T(8,128)(2,1)}), bf16[16,8,768]{2,1,0:T(8,128)(2,1)S(1)}, u32[]{:S(2)}, u32[]{:S(2)}) %all-to-all-start.1) | async-done | bytes 196640 | tf_op jit(solution)/shard_map/all_to_all | solution.py:85
  80.0 1.7 scatter_custom_fusion.2
  81.7 3.5 all-to-all-start.2
  85.5 2.0 fusion.72
  87.4 7.9 %all-to-all-done.2 = bf16[16,8,768]{2,1,0:T(8,128)(2,1)S(1)} async-done(((bf16[16,8,768]{2,1,0:T(8,128)(2,1)}), bf16[16,8,768]{2,1,0:T(8,128)(2,1)S(1)}, u32[]{:S(2)}, u32[]{:S(2)}) %all-to-all-start.2) | async-done | bytes 196640 | tf_op jit(solution)/shard_map/all_to_all | solution.py:107
  95.3 2.0 fusion.63
  97.3 218.4 %all-reduce.5.cloned.1.call-done = (f32[768,768]{1,0:T(8,128)}, f32[768,768]{1,0:T(8,128)}) async-done(((f32[768,768]{1,0:T(8,128)}, f32[768,768]{1,0:T(8,128)}), (f32[768,768]{1,0:T(8,128)}, f32[768,768]{1,0:T(8,128)})) %all-reduce.5.cloned.1.call-update) | async-done | bytes 4718608 | tf_op jit(solution)/shard_map/psum | solution.py:137
  317.1 1.8 fusion.74
  318.8 1.6 scatter_fusion
  321.0 2.0 scatter_fusion.1
  323.0 2.6 fusion.6
  325.6 1.6 collective-permute-start.2
  327.2 2.4 fusion.18
  329.6 4.5 collective-permute-start.3
  334.2 2.4 fusion.26
  338.7 2.4 add_add_fusion
  341.1 2.5 reshape.233
  343.6 3.6 reduce_sum.35
  347.2 125.7 %all-reduce.7.cloned.1.call-done = (f32[768,768]{1,0:T(8,128)}, f32[768,768]{1,0:T(8,128)}) async-done(((f32[768,768]{1,0:T(8,128)}, f32[768,768]{1,0:T(8,128)}), (f32[768,768]{1,0:T(8,128)}, f32[768,768]{1,0:T(8,128)})) %all-reduce.7.cloned.1.call-update) | async-done | bytes 4718608 | tf_op jit(solution)/shard_map/psum | solution.py:137
  472.9 1.7 dynamic-slice_multiply_fusion
  (66 shorter events, 20.0 us)
Async XLA Ops:
  7.2 53.5 %copy-start = (bf16[768,768]{1,0:T(8,128)(2,1)S(1)}, bf16[768,768]{1,0:T(8,128)(2,1)}, u32[]{:S(2)}) copy-start(bf16[768,768]{1,0:T(8,128)(2,1)} %param.14) | copy-start | bytes 3538948
  8.0 29.4 %collective-permute-start = (bf16[1,1,1024]{2,1,0:T(2,128)(2,1)S(1)}, bf16[1,1,1024]{2,1,0:T(2,128)(2,1)S(1)}, u32[]{:S(2)}, u32[]{:S(2)}) collective-permute-start(bf16[1,1,1024]{2,1,0:T(2,128)(2,1)S(1)} %get-tuple-element.12), channel_id=1, source_target_pairs={{0,1},{1,2},{2,3},{3,4},{4,5},{5,6},{6,7},{7,8},{8,9},{9,10},{10,1... | collective-permute-start | bytes 6152 | tf_op jit(solution)/shard_map/ppermute | solution.py:18
  11.5 26.0 %collective-permute-start.1 = (bf16[1,1,1024]{2,1,0:T(2,128)(2,1)S(1)}, bf16[1,1,1024]{2,1,0:T(2,128)(2,1)S(1)}, u32[]{:S(2)}, u32[]{:S(2)}) collective-permute-start(bf16[1,1,1024]{2,1,0:T(2,128)(2,1)S(1)} %get-tuple-element.13), channel_id=1, source_target_pairs={{1,0},{2,1},{3,2},{4,3},{5,4},{6,5},{7,6},{8,7},{9,8},{10,9},{11,1... | collective-permute-start | bytes 6152 | tf_op jit(solution)/shard_map/ppermute | solution.py:20
  14.5 52.6 %copy-start.8 = (s32[64]{0:T(128)}, s32[64]{0:T(128)S(1)}, u32[]{:S(2)}) copy-start(s32[64]{0:T(128)S(1)} %fusion.77) | copy-start | bytes 772
  16.0 20.2 %all-to-all-start = ((s32[16,1,8]{2,1,0:T(1,128)}), s32[16,1,8]{2,1,0:T(1,128)S(1)}, u32[]{:S(2)}, u32[]{:S(2)}) async-start(s32[16,1,8]{2,1,0:T(1,128)} %bitcast.16), calls=%async_computation | async-start | bytes 16384 | tf_op jit(solution)/shard_map/all_to_all | solution.py:79
  29.8 7.7 %copy-start.1 = (bf16[1,256,1024]{2,1,0:T(8,128)(2,1)S(1)}, bf16[1,256,1024]{2,1,0:T(8,128)(2,1)}, u32[]{:S(2)}) copy-start(bf16[1,256,1024]{2,1,0:T(8,128)(2,1)} %param.10) | copy-start | bytes 1572868
  39.6 4.0 copy-start.4
  49.1 3.6 copy-start.3
  60.7 17.4 %copy-start.2 = (bf16[768,768]{1,0:T(8,128)(2,1)S(1)}, bf16[768,768]{1,0:T(8,128)(2,1)}, u32[]{:S(2)}) copy-start(bf16[768,768]{1,0:T(8,128)(2,1)} %param.13) | copy-start | bytes 3538948
  61.7 15.7 %all-to-all-start.1 = ((bf16[16,8,768]{2,1,0:T(8,128)(2,1)}), bf16[16,8,768]{2,1,0:T(8,128)(2,1)S(1)}, u32[]{:S(2)}, u32[]{:S(2)}) async-start(bf16[16,8,768]{2,1,0:T(8,128)(2,1)} %fusion.40), calls=%async_computation.1 | async-start | bytes 393216 | tf_op jit(solution)/shard_map/all_to_all | solution.py:85
  69.1 10.3 %copy-start.6 = (f32[1,64]{1,0:T(1,128)S(1)}, f32[1,64]{1,0:T(1,128)}, u32[]{:S(2)}) copy-start(f32[1,64]{1,0:T(1,128)} %param.16) | copy-start | bytes 772
  69.1 10.3 %copy-start.7 = (s32[1,64]{1,0:T(1,128)S(1)}, s32[1,64]{1,0:T(1,128)}, u32[]{:S(2)}) copy-start(s32[1,64]{1,0:T(1,128)} %param.19) | copy-start | bytes 772
  77.4 8.1 %copy-start.5 = (bf16[64,768]{1,0:T(8,128)(2,1)S(1)}, bf16[64,768]{1,0:T(8,128)(2,1)}, u32[]{:S(2)}) copy-start(bf16[64,768]{1,0:T(8,128)(2,1)} %gather_fusion) | copy-start | bytes 294916
  81.7 13.6 %all-to-all-start.2 = ((bf16[16,8,768]{2,1,0:T(8,128)(2,1)}), bf16[16,8,768]{2,1,0:T(8,128)(2,1)S(1)}, u32[]{:S(2)}, u32[]{:S(2)}) async-start(bf16[16,8,768]{2,1,0:T(8,128)(2,1)} %bitcast.23), calls=%async_computation.2 | async-start | bytes 393216 | tf_op jit(solution)/shard_map/all_to_all | solution.py:107
  85.2 230.6 %all-reduce.5.cloned.1.call-start = ((), (), s32[]{:S(2)}) async-start(), calls=%async_computation.3 | async-start | bytes 9437184 | tf_op jit(solution)/shard_map/psum | solution.py:137
  97.3 375.6 %all-reduce.7.cloned.1.call-start = ((), (), s32[]{:S(2)}) async-start(), calls=%async_computation.4 | async-start | bytes 9437184 | tf_op jit(solution)/shard_map/psum | solution.py:137
  323.0 13.7 %slice-start = ((s8[7864320]{0:T(1024)(128)(4,1)}), s8[4194304]{0:T(1024)(128)(4,1)S(1)}, s32[]{:S(2)}) async-start(s8[7864320]{0:T(1024)(128)(4,1)} %bitcast.130), calls=%async_computation.5 | async-start | bytes 8388608
  325.6 11.0 %slice-start.1 = ((s8[7864320]{0:T(1024)(128)(4,1)}), s8[3670016]{0:T(1024)(128)(4,1)S(1)}, s32[]{:S(2)}) async-start(s8[7864320]{0:T(1024)(128)(4,1)} %bitcast.130), calls=%async_computation.6 | async-start | bytes 7340032
  325.6 8.5 %collective-permute-start.2 = (bf16[1,2,768]{2,1,0:T(2,128)(2,1)S(1)}, bf16[1,2,768]{2,1,0:T(2,128)(2,1)S(1)}, u32[]{:S(2)}, u32[]{:S(2)}) collective-permute-start(bf16[1,2,768]{2,1,0:T(2,128)(2,1)S(1)} %get-tuple-element.8), channel_id=1, source_target_pairs={{1,0},{2,1},{3,2},{4,3},{5,4},{6,5},{7,6},{8,7},{9,8},{10,9},{11,1... | collective-permute-start | bytes 9224 | tf_op jit(solution)/shard_map/ppermute | solution.py:20
  329.6 8.1 %collective-permute-start.3 = (bf16[1,2,768]{2,1,0:T(2,128)(2,1)S(1)}, bf16[1,2,768]{2,1,0:T(2,128)(2,1)S(1)}, u32[]{:S(2)}, u32[]{:S(2)}) collective-permute-start(bf16[1,2,768]{2,1,0:T(2,128)(2,1)S(1)} %get-tuple-element.9), channel_id=1, source_target_pairs={{0,1},{1,2},{2,3},{3,4},{4,5},{5,6},{6,7},{7,8},{8,9},{9,10},{10,1... | collective-permute-start | bytes 9224 | tf_op jit(solution)/shard_map/ppermute | solution.py:18
Sparse Core Ops, SparseCore 0:
  97.4 218.3 all-reduce.4
  318.5 154.3 all-reduce.6
